TPU v7x, 32 devices: a whole 2x2x4 slice. The times are simulated.
32 devices in a mesh: groups: 2 (over x), mp: 16 (over z, y, core).
Axes of the slice: x: 2, y: 2, z: 4, core: 2. Of those that a mesh axis runs over, the one named last changes fastest.
Arguments:
- up_pre: bfloat16 [96, 36864], P(('groups', 'mp')), parts along dimension 0, may hold values from -6 to 6
- down_weight: bfloat16 [36864, 18432], P('mp'), may hold values from -0.03125 to 0.03125
Outputs:
- mixed: bfloat16 [96, 18432], P(('groups', 'mp')), parts along dimension 0
There are 2 independent parts, one for each index of `groups`. A program takes and returns all parts, laid end to end along the dimension named above; an argument that names none is the same for every part. Nothing has to cross between parts.
All inputs are finite; a program needn't handle non-finite values.
Results may differ from a plain program's by a relative error of at most 0.0049.
Values may be sent and summed in bfloat16 or wider, within the bound.
A program may use at most 192 MiB of HBM per device.

v0:
```python
import jax
import jax.numpy as jnp
from jax import lax
from jax.sharding import PartitionSpec as P


def squared_relu(up_vals):
    positive = jnp.maximum(up_vals.astype(jnp.float32), 0.0)
    return (positive * positive).astype(jnp.bfloat16)


def body(up_pre, down_weight):
    up_cols = lax.all_to_all(up_pre, "mp", split_axis=1, concat_axis=0, tiled=True)
    hidden = squared_relu(up_cols)
    summed = lax.psum_scatter(
        jnp.dot(hidden, down_weight, preferred_element_type=jnp.float32),
        "mp",
        scatter_dimension=0,
        tiled=True,
    )
    return summed.astype(jnp.bfloat16)


def solution(mesh):
    in_specs = (P(("groups", "mp"), None), P("mp", None))
    out_specs = P(("groups", "mp"), None)
    return jax.shard_map(body, mesh=mesh, in_specs=in_specs, out_specs=out_specs, check_vma=False)
```

profile of v0, /device:TPU:0, one launch (start us, length us, event | category | flops | bytes accessed | tf_op | source)
XLA Modules:
  0.0 133.7 jit_solution(9623923574776971299)
XLA Ops:
  0.0 7.4 %all-to-all-start = ((bf16[3,16,2304]{2,0,1:T(4,128)(2,1)}), bf16[3,16,2304]{2,0,1:T(4,128)(2,1)S(1)}, u32[]{:S(2)}, u32[]{:S(2)}) async-start(bf16[3,16,2304]{2,0,1:T(4,128)(2,1)} %bitcast.6), calls=%async_computation | async-start | bytes 589824 | tf_op jit(solution)/shard_map/all_to_all | solution.py:13
  7.4 1.2 dynamic-slice
  9.3 8.7 %all-to-all-done = bf16[3,16,2304]{2,0,1:T(4,128)(2,1)S(1)} async-done(((bf16[3,16,2304]{2,0,1:T(4,128)(2,1)}), bf16[3,16,2304]{2,0,1:T(4,128)(2,1)S(1)}, u32[]{:S(2)}, u32[]{:S(2)}) %all-to-all-start) | async-done | bytes 221216 | tf_op jit(solution)/shard_map/all_to_all | solution.py:13
  18.0 0.2 fusion
  18.1 0.9 convert_element_type.13
  19.0 29.2 %fusion.1 = f32[48,18432]{1,0:T(8,128)S(1)} fusion(bf16[48,2304]{1,0:T(8,128)(2,1)} %convert_element_type.13, bf16[2304,18432]{1,0:T(8,128)(2,1)} %param.3), kind=kOutput, calls=%fused_computation.3 | convolution fusion | flops 4076863488 | bytes 88694784 | tf_op jit(solution)/shard_map/dot_general | solution.py:16
  48.2 83.7 %all-reduce.2 = bf16[48,18432]{1,0:T(8,128)(2,1)} all-reduce(f32[48,18432]{1,0:T(8,128)S(1)} %fusion.1), channel_id=2, replica_groups=mesh['groups'=2,'mp'=16] {'mp'}, use_global_device_ids=true, to_apply=%region_0.0.clone | all-reduce | flops 884736 | bytes 5308416
  131.9 1.8 %dynamic-slice_convert_fusion = bf16[3,18432]{1,0:T(4,128)(2,1)} fusion(bf16[48,18432]{1,0:T(8,128)(2,1)} %all-reduce.2, u32[]{:T(128)S(6)} %multiply.1), kind=kLoop, calls=%fused_computation.2 | loop fusion | bytes 221188 | tf_op jit(solution)/shard_map/convert_element_type | solution.py:21
Async XLA Ops:
  0.0 18.0 %all-to-all-start = ((bf16[3,16,2304]{2,0,1:T(4,128)(2,1)}), bf16[3,16,2304]{2,0,1:T(4,128)(2,1)S(1)}, u32[]{:S(2)}, u32[]{:S(2)}) async-start(bf16[3,16,2304]{2,0,1:T(4,128)(2,1)} %bitcast.6), calls=%async_computation | async-start | bytes 589824 | tf_op jit(solution)/shard_map/all_to_all | solution.py:13
where the time goes:
time: 135 us; the launch traced here: 134 us
  blocking collectives  83.7 us (62%)
  matrix products  29.2 us (22%)
  waiting for transfers between devices  8.67 us (6%)
  starting transfers between devices  7.39 us (5%)
  local copies, waits for them, and re-layouts  3.92 us (3%)
    unnamed x1, blocking collectives  83.7 us
    dot_general x1, matrix products, body(): jnp.dot(hidden, down_weight, preferred_element_type=jnp.float32)  29.2 us
    all_to_all x1, waiting for transfers between devices, body(): lax.all_to_all(up_pre, 'mp', split_axis=1, concat_axis=0, tiled=True)  8.67 us
    all_to_all x1, starting transfers between devices, body(): lax.all_to_all(up_pre, 'mp', split_axis=1, concat_axis=0, tiled=True)  7.39 us
  transfers between devices with their start and end apart: 1, of which 1 were waited for; matrix products, arithmetic and copies ran while one was open for 1% of the time, Pallas kernels for 0%

commit v1 on v0

v1 whole, which is shorter than its diff:
```python
import functools

import jax
import jax.numpy as jnp
from jax import lax
from jax.experimental import pallas as pl
from jax.experimental.pallas import tpu as pltpu
from jax.sharding import PartitionSpec as P

MESH = pl.DeviceIdType.MESH


def squared_relu(up_vals):
    positive = jnp.maximum(up_vals.astype(jnp.float32), 0.0)
    return (positive * positive).astype(jnp.bfloat16)


def plain_body(up_pre, down_weight):
    up_cols = lax.all_to_all(up_pre, "mp", split_axis=1, concat_axis=0, tiled=True)
    hidden = squared_relu(up_cols)
    summed = lax.psum_scatter(
        jnp.dot(hidden, down_weight, preferred_element_type=jnp.float32),
        "mp",
        scatter_dimension=0,
        tiled=True,
    )
    return summed.astype(jnp.bfloat16)


def kernel(n, up_ref, w_ref, out_ref, wbuf, upbuf, hid32, hid, yb, asend, arecv, bsend, brecv, csend, crecv, own, fin,
           w_sem, up_ssem, up_rsem, own_sem, a_ssem, a_rsem, b_ssem, b_rsem, c_ssem, c_rsem, f_ssem, f_rsem, fl_sem):
    nz = n // 4
    chunks = n // 2
    x = lax.axis_index("groups")
    p = lax.axis_index("mp")
    me = x * n + p
    chip, core = p // 2, p % 2
    z, y = chip // 2, chip % 2
    rows, depth, width = up_ref.shape[0], w_ref.shape[0], wbuf.shape[2]
    group_rows = rows * n
    half = width * chunks

    def cols_of(x_part, chunk):
        return pl.ds(pl.multiple_of(x_part * half + chunk * width, 128), width)

    def chunk_of(t):
        zt = lax.rem(z + 1 + t // 2, nz)
        yt = jnp.where(t % 2 == 0, 1 - y, y)
        return zt * 2 + yt

    def w_copy(t):
        return pltpu.make_async_copy(w_ref.at[:, cols_of(x, chunk_of(t))], wbuf.at[t], w_sem.at[t])

    def start_w(t, _):
        w_copy(t).start()
        return 0

    lax.fori_loop(0, chunks, start_w, 0)

    barrier = pltpu.get_barrier_semaphore()

    def greet(d, _):
        other = lax.rem(me + d, 2 * n)
        pl.semaphore_signal(barrier, inc=1, device_id=(other // n, lax.rem(other, n)), device_id_type=MESH)
        return 0

    lax.fori_loop(1, 2 * n, greet, 0)

    def up_cols(q):
        return up_ref.at[:, pl.ds(pl.multiple_of(q * depth, 128), depth)]

    def up_copy(d, slot):
        other = lax.rem(me + d, 2 * n)
        q = lax.rem(other, n)
        return pltpu.make_async_remote_copy(
            src_ref=up_cols(q), dst_ref=upbuf.at[slot], send_sem=up_ssem.at[d], recv_sem=up_rsem.at[slot],
            device_id=(other // n, q), device_id_type=MESH)

    own_up = pltpu.make_async_copy(up_cols(p), upbuf.at[me], own_sem)
    own_up.start()
    pl.semaphore_wait(barrier, 2 * n - 1)

    def start_up(d, _):
        up_copy(d, me).start()
        return 0

    lax.fori_loop(1, 2 * n, start_up, 0)
    own_up.wait()

    def wait_up(d, _):
        up_copy(d, lax.rem(me + 2 * n - d, 2 * n)).wait_recv()
        return 0

    lax.fori_loop(1, 2 * n, wait_up, 0)
    for s in range(2 * n):
        positive = jnp.maximum(upbuf[s].astype(jnp.float32), 0.0)
        hid32[s * rows:(s + 1) * rows, :] = positive * positive
    hid[...] = hid32[...].astype(jnp.bfloat16)

    def a_copy(t):
        return pltpu.make_async_remote_copy(
            src_ref=asend.at[t], dst_ref=arecv.at[t], send_sem=a_ssem.at[t], recv_sem=a_rsem.at[t],
            device_id=(x, chip * 2 + 1 - core), device_id_type=MESH)

    def b_copy(j):
        return pltpu.make_async_remote_copy(
            src_ref=bsend.at[j], dst_ref=brecv.at[j], send_sem=b_ssem.at[j], recv_sem=b_rsem.at[j],
            device_id=(x, (z * 2 + 1 - y) * 2 + core), device_id_type=MESH)

    def c_copy(j):
        return pltpu.make_async_remote_copy(
            src_ref=csend.at[j], dst_ref=crecv.at[j], send_sem=c_ssem.at[j], recv_sem=c_rsem.at[j],
            device_id=(x, (lax.rem(z + 1 + j, nz) * 2 + y) * 2 + core), device_id_type=MESH)

    def step(t, _):
        @pl.when(t < chunks)
        def _():
            w_copy(t).wait()
            prod = jnp.dot(hid[...], wbuf[t], preferred_element_type=jnp.float32)
            yb[t % 2, 0] = prod[:group_rows]
            yb[t % 2, 1] = prod[group_rows:]
            asend[t] = yb[t % 2, 1 - core].astype(jnp.bfloat16)
            a_copy(t).start()

        @pl.when(t >= 1)
        def _():
            u = t - 1
            j = u // 2
            a_copy(u).wait_recv()
            total = yb[u % 2, core] + arecv[u].astype(jnp.float32)

            @pl.when(u % 2 == 0)
            def _():
                bsend[j] = total.astype(jnp.bfloat16)
                b_copy(j).start()

            @pl.when(u % 2 == 1)
            def _():
                b_copy(j).wait_recv()
                both = total + brecv[j].astype(jnp.float32)

                @pl.when(j < nz - 1)
                def _():
                    csend[j] = both.astype(jnp.bfloat16)
                    c_copy(j).start()

                @pl.when(j == nz - 1)
                def _():
                    own[...] = both

        return 0

    lax.fori_loop(0, chunks + 1, step, 0)

    for j in range(nz - 1):
        c_copy(j).wait_recv()
    total = own[...]
    for j in range(nz - 1):
        total = total + crecv[j].astype(jnp.float32)
    for q in range(n):
        fin[q] = total[q * rows:(q + 1) * rows].astype(jnp.bfloat16)

    def f_copy(q, x_part, chunk):
        return pltpu.make_async_remote_copy(
            src_ref=fin.at[q], dst_ref=out_ref.at[:, cols_of(x_part, chunk)], send_sem=f_ssem.at[q],
            recv_sem=f_rsem.at[x_part * chunks + chunk], device_id=(core, q), device_id_type=MESH)

    mine = pltpu.make_async_copy(fin.at[p], out_ref.at[:, cols_of(x, chip)], fl_sem)

    @pl.when(x == core)
    def _():
        mine.start()

    def each_final(q, act):
        @pl.when(jnp.logical_or(x != core, q != p))
        def _():
            act(f_copy(q, x, chip))

    def start_final(i, _):
        each_final(lax.rem(p + i, n), lambda c: c.start())
        return 0

    lax.fori_loop(0, n, start_final, 0)

    def wait_final(i, _):
        x_part, chunk = i // chunks, lax.rem(i, chunks)

        @pl.when(jnp.logical_or(x_part != x, chunk * 2 + x != p))
        def _():
            f_copy(i, x_part, chunk).wait_recv()

        return 0

    lax.fori_loop(0, n, wait_final, 0)

    @pl.when(x == core)
    def _():
        mine.wait()

    def end_up(d, _):
        up_copy(d, me).wait_send()
        return 0

    def end_a(t, _):
        a_copy(t).wait_send()
        return 0

    def end_final(q, _):
        each_final(q, lambda c: c.wait_send())
        return 0

    lax.fori_loop(1, 2 * n, end_up, 0)
    lax.fori_loop(0, chunks, end_a, 0)
    for j in range(nz):
        b_copy(j).wait_send()
    for j in range(nz - 1):
        c_copy(j).wait_send()
    lax.fori_loop(0, n, end_final, 0)


def fused_body(n, up_pre, down_weight):
    rows = up_pre.shape[0]
    depth, model = down_weight.shape
    nz, chunks, tokens = n // 4, n // 2, rows * n
    width = model // n
    bf, f32, dma = jnp.bfloat16, jnp.float32, pltpu.SemaphoreType.DMA
    return pl.pallas_call(
        functools.partial(kernel, n),
        out_shape=jax.ShapeDtypeStruct((rows, model), bf),
        in_specs=[pl.BlockSpec(memory_space=pl.ANY)] * 2,
        out_specs=pl.BlockSpec(memory_space=pl.ANY),
        scratch_shapes=[
            pltpu.VMEM((chunks, depth, width), bf),
            pltpu.VMEM((2 * n, rows, depth), bf),
            pltpu.VMEM((2 * tokens, depth), f32),
            pltpu.VMEM((2 * tokens, depth), bf),
            pltpu.VMEM((2, 2, tokens, width), f32),
            pltpu.VMEM((chunks, tokens, width), bf),
            pltpu.VMEM((chunks, tokens, width), bf),
            pltpu.VMEM((nz, tokens, width), bf),
            pltpu.VMEM((nz, tokens, width), bf),
            pltpu.VMEM((nz - 1, tokens, width), bf),
            pltpu.VMEM((nz - 1, tokens, width), bf),
            pltpu.VMEM((tokens, width), f32),
            pltpu.VMEM((n, rows, width), bf),
            dma((chunks,)), dma((2 * n,)), dma((2 * n,)), dma,
            dma((chunks,)), dma((chunks,)), dma((nz,)), dma((nz,)), dma((nz - 1,)), dma((nz - 1,)),
            dma((n,)), dma((n,)), dma,
        ],
        compiler_params=pltpu.CompilerParams(collective_id=0, has_side_effects=True, vmem_limit_bytes=60 * 2 ** 20),
        cost_estimate=pl.CostEstimate(flops=4 * tokens * depth * model // 2, bytes_accessed=depth * model, transcendentals=0),
    )(up_pre, down_weight)


def solution(mesh):
    in_specs = (P(("groups", "mp"), None), P("mp", None))
    out_specs = P(("groups", "mp"), None)
    n = mesh.shape["mp"]

    def body(up_pre, down_weight):
        depth, model = down_weight.shape
        resident = depth * model
        fits = mesh.shape["groups"] == 2 and n == 16 and (up_pre.shape[0] * n) % 16 == 0
        if fits and model % (128 * n) == 0 and depth % 128 == 0 and resident <= 44 * 2 ** 20:
            return fused_body(n, up_pre, down_weight)
        return plain_body(up_pre, down_weight)

    return jax.shard_map(body, mesh=mesh, in_specs=in_specs, out_specs=out_specs, check_vma=False)
```

time: 135 us -> 53.9 us (0.40)
  blocking collectives: 83.7 us -> 0 us
  Pallas kernels: 0 us -> 52.1 us
  matrix products: 29.2 us -> 0 us
  waiting for transfers between devices: 8.67 us -> 0 us
  starting transfers between devices: 7.39 us -> 0 us
  local copies, waits for them, and re-layouts: 3.92 us -> 1.62 us
    unnamed x1 -> x0, blocking collectives: 83.7 us -> none
    pallas_call x0 -> x1, Pallas kernels: none -> 52.1 us  [fused_body(): pl.pallas_call(functools.partial(kernel, n), out_shape=jax.ShapeDtypeStru...]
    dot_general x1 -> x0, matrix products: 29.2 us -> none  [body(): jnp.dot(hidden, down_weight, preferred_element_type=jnp.float32)]
    all_to_all x1 -> x0, waiting for transfers between devices: 8.67 us -> none  [body(): lax.all_to_all(up_pre, 'mp', split_axis=1, concat_axis=0, tiled=True)]
    all_to_all x1 -> x0, starting transfers between devices: 7.39 us -> none  [body(): lax.all_to_all(up_pre, 'mp', split_axis=1, concat_axis=0, tiled=True)]
    convert_element_type x2 -> x0, local copies, waits for them, and re-layouts: 2.68 us -> none  [the longest x1 1.82 us: body(): return summed.astype(jnp.bfloat16)]
  transfers between devices with their start and end apart: 1 -> 0, of which waited for: 1 -> 0; matrix products, arithmetic and copies ran while one was open for 1% -> 0% of each run, Pallas kernels for 0% -> 0%
where the time goes in v1:
time: 53.9 us; the launch traced here: 53.7 us
  Pallas kernels  52.1 us (97%)
  local copies, waits for them, and re-layouts  1.62 us (3%)
    pallas_call x1, Pallas kernels, fused_body(): pl.pallas_call(functools.partial(kernel, n), out_shape=jax.ShapeDtypeStru...  52.1 us
    unnamed x1, local copies, waits for them, and re-layouts  1.62 us

profile of v1, /device:TPU:0, one launch (start us, length us, event | category | flops | bytes accessed | tf_op | source)
XLA Modules:
  0.0 53.7 jit_solution(7568732509004617492)
XLA Ops:
  0.0 52.1 %shard_map.28 = bf16[3,18432]{1,0:T(4,128)(2,1)} custom-call(bf16[3,36864]{1,0:T(4,128)(2,1)} %up_ref.1, bf16[2304,18432]{1,0:T(8,128)(2,1)} %w_ref.1), custom_call_target="tpu_custom_call" | custom-call | flops 4076863488 | bytes 42467328 | tf_op jit(solution)/shard_map/pallas_call | solution.py:227
  52.1 1.6 %copy.4 = bf16[3,18432]{1,0:T(4,128)(2,1)} copy(bf16[3,18432]{1,0:T(4,128)(2,1)} %shard_map.28) | data formatting | bytes 221184

commit v2 on v1

--- a/solution.py
+++ b/solution.py
@@ -8,6 +8,7 @@
 from jax.sharding import PartitionSpec as P
 
 MESH = pl.DeviceIdType.MESH
+LAG_A, LAG_B = 1, 2
 
 
 def squared_relu(up_vals):
@@ -27,8 +28,8 @@
     return summed.astype(jnp.bfloat16)
 
 
-def kernel(n, up_ref, w_ref, out_ref, wbuf, upbuf, hid32, hid, yb, asend, arecv, bsend, brecv, csend, crecv, own, fin,
-           w_sem, up_ssem, up_rsem, own_sem, a_ssem, a_rsem, b_ssem, b_rsem, c_ssem, c_rsem, f_ssem, f_rsem, fl_sem):
+def kernel(n, up_ref, w_ref, out_ref, wbuf, upbuf, hid32, hid, ykeep, asend, arecv, bkeep, bsend, brecv, csend, crecv, own, fin,
+           w_sem, up_ssem, up_rsem, fw_ssem, fw_rsem, own_sem, a_ssem, a_rsem, b_ssem, b_rsem, c_ssem, c_rsem, f_ssem, f_rsem, fl_sem):
     nz = n // 4
     chunks = n // 2
     x = lax.axis_index("groups")
@@ -70,32 +71,46 @@
         return up_ref.at[:, pl.ds(pl.multiple_of(q * depth, 128), depth)]
 
     def up_copy(d, slot):
-        other = lax.rem(me + d, 2 * n)
-        q = lax.rem(other, n)
-        return pltpu.make_async_remote_copy(
-            src_ref=up_cols(q), dst_ref=upbuf.at[slot], send_sem=up_ssem.at[d], recv_sem=up_rsem.at[slot],
-            device_id=(other // n, q), device_id_type=MESH)
-
-    own_up = pltpu.make_async_copy(up_cols(p), upbuf.at[me], own_sem)
+        q = lax.rem(p + d, n)
+        return pltpu.make_async_remote_copy(
+            src_ref=up_cols(q), dst_ref=upbuf.at[0, slot], send_sem=up_ssem.at[d], recv_sem=up_rsem.at[slot],
+            device_id=(x, q), device_id_type=MESH)
+
+    def forward(s):
+        return pltpu.make_async_remote_copy(
+            src_ref=upbuf.at[0, s], dst_ref=upbuf.at[1, s], send_sem=fw_ssem.at[s], recv_sem=fw_rsem.at[s],
+            device_id=(1 - x, p), device_id_type=MESH)
+
+    own_up = pltpu.make_async_copy(up_cols(p), upbuf.at[0, p], own_sem)
     own_up.start()
     pl.semaphore_wait(barrier, 2 * n - 1)
 
     def start_up(d, _):
-        up_copy(d, me).start()
-        return 0
-
-    lax.fori_loop(1, 2 * n, start_up, 0)
+        up_copy(d, p).start()
+        return 0
+
+    lax.fori_loop(1, n, start_up, 0)
     own_up.wait()
-
-    def wait_up(d, _):
-        up_copy(d, lax.rem(me + 2 * n - d, 2 * n)).wait_recv()
-        return 0
-
-    lax.fori_loop(1, 2 * n, wait_up, 0)
-    for s in range(2 * n):
-        positive = jnp.maximum(upbuf[s].astype(jnp.float32), 0.0)
-        hid32[s * rows:(s + 1) * rows, :] = positive * positive
-    hid[...] = hid32[...].astype(jnp.bfloat16)
+    forward(p).start()
+
+    def pass_on(d, _):
+        s = lax.rem(p + n - d, n)
+        up_copy(d, s).wait_recv()
+        forward(s).start()
+        return 0
+
+    lax.fori_loop(1, n, pass_on, 0)
+    for part in range(2):
+        if part == 1:
+            for s in range(n):
+                forward(s).wait_recv()
+        for s in range(n):
+            row = part * group_rows + s * rows
+            positive = jnp.maximum(upbuf[part, s].astype(jnp.float32), 0.0)
+            hid32[row:row + rows, :] = positive * positive
+        span = slice(part * group_rows, (part + 1) * group_rows)
+        hid[span, :] = hid32[span, :].astype(jnp.bfloat16)
+    keep = lax.rem(x + core, 2)
 
     def a_copy(t):
         return pltpu.make_async_remote_copy(
@@ -117,17 +132,18 @@
         def _():
             w_copy(t).wait()
             prod = jnp.dot(hid[...], wbuf[t], preferred_element_type=jnp.float32)
-            yb[t % 2, 0] = prod[:group_rows]
-            yb[t % 2, 1] = prod[group_rows:]
-            asend[t] = yb[t % 2, 1 - core].astype(jnp.bfloat16)
+            ykeep[t, 0] = prod[:group_rows]
+            ykeep[t, 1] = prod[group_rows:]
+            asend[t] = ykeep[t, 1 - keep].astype(jnp.bfloat16)
             a_copy(t).start()
 
-        @pl.when(t >= 1)
-        def _():
-            u = t - 1
+        u = t - LAG_A
+
+        @pl.when(jnp.logical_and(u >= 0, u < chunks))
+        def _():
+            a_copy(u).wait_recv()
+            total = ykeep[u, keep] + arecv[u].astype(jnp.float32)
             j = u // 2
-            a_copy(u).wait_recv()
-            total = yb[u % 2, core] + arecv[u].astype(jnp.float32)
 
             @pl.when(u % 2 == 0)
             def _():
@@ -136,21 +152,28 @@
 
             @pl.when(u % 2 == 1)
             def _():
-                b_copy(j).wait_recv()
-                both = total + brecv[j].astype(jnp.float32)
-
-                @pl.when(j < nz - 1)
-                def _():
-                    csend[j] = both.astype(jnp.bfloat16)
-                    c_copy(j).start()
-
-                @pl.when(j == nz - 1)
-                def _():
-                    own[...] = both
-
-        return 0
-
-    lax.fori_loop(0, chunks + 1, step, 0)
+                bkeep[j] = total
+
+        v = t - LAG_A - LAG_B
+
+        @pl.when(jnp.logical_and(v >= 0, v % 2 == 1))
+        def _():
+            j = v // 2
+            b_copy(j).wait_recv()
+            both = bkeep[j] + brecv[j].astype(jnp.float32)
+
+            @pl.when(j < nz - 1)
+            def _():
+                csend[j] = both.astype(jnp.bfloat16)
+                c_copy(j).start()
+
+            @pl.when(j == nz - 1)
+            def _():
+                own[...] = both
+
+        return 0
+
+    lax.fori_loop(0, chunks + LAG_A + LAG_B, step, 0)
 
     for j in range(nz - 1):
         c_copy(j).wait_recv()
@@ -198,7 +221,7 @@
         mine.wait()
 
     def end_up(d, _):
-        up_copy(d, me).wait_send()
+        up_copy(d, p).wait_send()
         return 0
 
     def end_a(t, _):
@@ -209,7 +232,9 @@
         each_final(q, lambda c: c.wait_send())
         return 0
 
-    lax.fori_loop(1, 2 * n, end_up, 0)
+    lax.fori_loop(1, n, end_up, 0)
+    for s in range(n):
+        forward(s).wait_send()
     lax.fori_loop(0, chunks, end_a, 0)
     for j in range(nz):
         b_copy(j).wait_send()
@@ -231,19 +256,20 @@
         out_specs=pl.BlockSpec(memory_space=pl.ANY),
         scratch_shapes=[
             pltpu.VMEM((chunks, depth, width), bf),
-            pltpu.VMEM((2 * n, rows, depth), bf),
+            pltpu.VMEM((2, n, rows, depth), bf),
             pltpu.VMEM((2 * tokens, depth), f32),
             pltpu.VMEM((2 * tokens, depth), bf),
-            pltpu.VMEM((2, 2, tokens, width), f32),
+            pltpu.VMEM((chunks, 2, tokens, width), f32),
             pltpu.VMEM((chunks, tokens, width), bf),
             pltpu.VMEM((chunks, tokens, width), bf),
+            pltpu.VMEM((nz, tokens, width), f32),
             pltpu.VMEM((nz, tokens, width), bf),
             pltpu.VMEM((nz, tokens, width), bf),
             pltpu.VMEM((nz - 1, tokens, width), bf),
             pltpu.VMEM((nz - 1, tokens, width), bf),
             pltpu.VMEM((tokens, width), f32),
             pltpu.VMEM((n, rows, width), bf),
-            dma((chunks,)), dma((2 * n,)), dma((2 * n,)), dma,
+            dma((chunks,)), dma((n,)), dma((n,)), dma((n,)), dma((n,)), dma,
             dma((chunks,)), dma((chunks,)), dma((nz,)), dma((nz,)), dma((nz - 1,)), dma((nz - 1,)),
             dma((n,)), dma((n,)), dma,
         ],

time: 53.9 us -> 50.5 us (0.937)
  Pallas kernels: 52.1 us -> 48.8 us
    pallas_call x1, Pallas kernels: 52.1 us -> 48.8 us  [fused_body(): pl.pallas_call(functools.partial(kernel, n), out_shape=jax.ShapeDtypeStru...]
where the time goes in v2:
time: 50.5 us; the launch traced here: 50.4 us
  Pallas kernels  48.8 us (97%)
  local copies, waits for them, and re-layouts  1.62 us (3%)
    pallas_call x1, Pallas kernels, fused_body(): pl.pallas_call(functools.partial(kernel, n), out_shape=jax.ShapeDtypeStru...  48.8 us
    unnamed x1, local copies, waits for them, and re-layouts  1.62 us

profile of v2, /device:TPU:0, one launch (start us, length us, event | category | flops | bytes accessed | tf_op | source)
XLA Modules:
  0.0 50.4 jit_solution(8961503388461324891)
XLA Ops:
  0.0 48.8 %shard_map.28 = bf16[3,18432]{1,0:T(4,128)(2,1)} custom-call(bf16[3,36864]{1,0:T(4,128)(2,1)} %up_ref.1, bf16[2304,18432]{1,0:T(8,128)(2,1)} %w_ref.1), custom_call_target="tpu_custom_call" | custom-call | flops 4076863488 | bytes 42467328 | tf_op jit(solution)/shard_map/pallas_call | solution.py:252
  48.8 1.6 %copy.4 = bf16[3,18432]{1,0:T(4,128)(2,1)} copy(bf16[3,18432]{1,0:T(4,128)(2,1)} %shard_map.28) | data formatting | bytes 221184

commit v3 on v2

--- a/solution.py
+++ b/solution.py
@@ -9,6 +9,7 @@
 
 MESH = pl.DeviceIdType.MESH
 LAG_A, LAG_B = 1, 2
+EARLY = 4
 
 
 def squared_relu(up_vals):
@@ -56,7 +57,7 @@
         w_copy(t).start()
         return 0
 
-    lax.fori_loop(0, chunks, start_w, 0)
+    lax.fori_loop(0, EARLY, start_w, 0)
 
     barrier = pltpu.get_barrier_semaphore()
 
@@ -100,6 +101,7 @@
         return 0
 
     lax.fori_loop(1, n, pass_on, 0)
+    lax.fori_loop(EARLY, chunks, start_w, 0)
     for part in range(2):
         if part == 1:
             for s in range(n):

time: 50.5 us -> 45.4 us (0.90)
  Pallas kernels: 48.8 us -> 43.6 us
    pallas_call x1, Pallas kernels: 48.8 us -> 43.6 us  [fused_body(): pl.pallas_call(functools.partial(kernel, n), out_shape=jax.ShapeDtypeStru...]
where the time goes in v3:
time: 45.4 us; the launch traced here: 45.2 us
  Pallas kernels  43.6 us (96%)
  local copies, waits for them, and re-layouts  1.62 us (4%)
    pallas_call x1, Pallas kernels, fused_body(): pl.pallas_call(functools.partial(kernel, n), out_shape=jax.ShapeDtypeStru...  43.6 us
    unnamed x1, local copies, waits for them, and re-layouts  1.62 us

profile of v3, /device:TPU:0, one launch (start us, length us, event | category | flops | bytes accessed | tf_op | source)
XLA Modules:
  0.0 45.2 jit_solution(10942927554681642998)
XLA Ops:
  0.0 43.6 %shard_map.28 = bf16[3,18432]{1,0:T(4,128)(2,1)} custom-call(bf16[3,36864]{1,0:T(4,128)(2,1)} %up_ref.1, bf16[2304,18432]{1,0:T(8,128)(2,1)} %w_ref.1), custom_call_target="tpu_custom_call" | custom-call | flops 4076863488 | bytes 42467328 | tf_op jit(solution)/shard_map/pallas_call | solution.py:254
  43.6 1.6 %copy.4 = bf16[3,18432]{1,0:T(4,128)(2,1)} copy(bf16[3,18432]{1,0:T(4,128)(2,1)} %shard_map.28) | data formatting | bytes 221184
